TPU v7x, 512 devices: a whole 4x8x8 slice. The times are simulated.
512 devices in a mesh: frames: 8 (over x, core), atoms: 64 (over z, y).
Axes of the slice: x: 4, y: 8, z: 8, core: 2. Of those that a mesh axis runs over, the one named last changes fastest.
Arguments:
- coords: bfloat16 [8, 3, 4194304], P('frames', None, 'atoms'), may hold values from -32 to 32, as said below
- reference_structure: float32 [3, 4194304], P(None, 'atoms'), may hold values from -8 to 8
Outputs:
- mean_structure: float32 [3, 4194304], P(None, 'atoms')
- transforms: float32 [8, 12], P('frames')
Inputs may be any that keep to these rules, and one draw needn't show every extreme that they name: `coords`: every frame is a perturbed affine image of one common structure plus independent per-atom displacements.
All inputs are finite; a program needn't handle non-finite values.
Results may differ from a plain program's by a relative error of at most 0.0003.
Values may be sent and summed in bfloat16 or wider, within the bound.
A program may use at most 128 MiB of HBM per device.

v0:
```python
import jax
import jax.numpy as jnp
from jax import lax
from jax.sharding import PartitionSpec as P

ITERS = 2


highest = lax.Precision.HIGHEST
eps = 1e-06


def gram_terms(positions):
    inner = jnp.einsum("fia,fja->fij", positions, positions, preferred_element_type=jnp.float32)
    row_sums = jnp.sum(positions, axis=2, dtype=jnp.float32)
    frame_total = positions.shape[0]
    counted = jnp.full((frame_total, 1), float(positions.shape[2]), jnp.float32)
    upper = jnp.concatenate([inner, row_sums[:, :, None]], axis=2)
    lower = jnp.concatenate([row_sums, counted], axis=1)[:, None, :]
    return jnp.concatenate([upper, lower], axis=1)


def cross_terms(structure, positions):
    linear = jnp.einsum(
        "ia,fja->fij", structure, positions, precision=highest, preferred_element_type=jnp.float32
    )
    offsets = jnp.sum(structure, axis=1)
    offsets = offsets[None, :, None]
    return jnp.concatenate([linear, offsets], axis=2)


def apply_maps(affine_maps, positions):
    moved = jnp.einsum(
        "fij,fja->ia",
        affine_maps[:, :, :3],
        positions,
        precision=highest,
        preferred_element_type=jnp.float32,
    )
    return moved + jnp.sum(affine_maps[:, :, 3], axis=0)[:, None]


def solve_one(cross, gram):
    factor = jnp.linalg.cholesky(gram)
    return jax.scipy.linalg.cho_solve((factor, True), cross.T).T


def run_iterations(
    positions, structure, atom_count, mean_of, first_sums, centroid_sums, spread_sums, moment_sums
):
    gram, cross = first_sums(gram_terms(positions), cross_terms(structure, positions))
    affine_maps = None
    for step in range(ITERS):
        affine_maps = jax.vmap(solve_one)(cross, gram)
        mean_raw = mean_of(apply_maps(affine_maps, positions))
        centre = centroid_sums(jnp.sum(mean_raw, axis=1)) / atom_count
        shifted = mean_raw - centre[:, None]
        squares = spread_sums(jnp.sum(shifted * shifted))
        structure = shifted / jnp.sqrt(squares / atom_count + eps)
        if step + 1 < ITERS:
            cross = moment_sums(cross_terms(structure, positions))
    return (structure, affine_maps)


def per_device(coords, reference_structure):
    own_frames = coords.shape[0]
    frame_count = own_frames * lax.axis_size("frames")
    atom_count = coords.shape[2] * lax.axis_size("atoms")
    structure, affine_maps = run_iterations(
        coords,
        reference_structure,
        atom_count,
        lambda partial_sum: lax.psum(partial_sum, "frames") / frame_count,
        lambda gram_part, cross_part: lax.psum((gram_part, cross_part), "atoms"),
        lambda first: lax.psum(first, "atoms"),
        lambda first: lax.psum(first, "atoms"),
        lambda first: lax.psum(first, "atoms"),
    )
    return (structure, affine_maps.reshape(own_frames, 12))


def solution(mesh):
    in_specs = (P("frames", None, "atoms"), P(None, "atoms"))
    out_specs = (P(None, "atoms"), P("frames", None))
    return jax.shard_map(
        per_device, mesh=mesh, in_specs=in_specs, out_specs=out_specs, check_vma=False
    )
```

profile of v0, /device:TPU:8, one launch (start us, length us, event | category | flops | bytes accessed | tf_op | source)
XLA Modules:
  0.0 1025.1 jit_solution(10395784185505046742)
XLA Ops:
  7.2 0.0 copy-start.2
  7.2 0.0 all-reduce.4.cloned.1.call-start
  7.2 1.7 convert_reduce_fusion
  9.0 0.0 copy-done.2
  9.0 0.8 convolution_bitcast_fusion.2
  9.7 0.0 copy-start.3
  9.7 3.7 convolution_bitcast_fusion.4
  13.4 0.0 copy-done.3
  13.4 0.7 reduce_sum.75
  14.1 0.1 maximum_bitcast_fusion.2
  14.2 0.1 copy.17
  14.3 0.1 pad_maximum_fusion
  14.3 146.3 %all-reduce = (f32[1,4,4]{1,2,0:T(4,128)S(1)}, f32[1,4,3]{2,1,0:T(4,128)S(1)}) all-reduce(f32[1,4,4]{1,2,0:T(4,128)S(1)} %pad_maximum_fusion, f32[1,4,3]{2,1,0:T(4,128)S(1)} %maximum_bitcast_fusion), channel_id=1, replica_groups=mesh['frames'=8,'atoms'=64] {'atoms'}, use_global_device_ids=true, to_apply=%region_1.0 | all-reduce | flops 28 | bytes 224 | tf_op jit(solution)/shard_map/psum | solution.py:74
  160.7 0.1 copy.18
  160.8 0.4 custom-call.9
  161.2 0.6 compare_reduce_fusion
  161.8 0.6 fusion.5
  162.5 0.3 custom-call.11
  162.8 0.2 fusion.7
  163.0 0.1 convolution_bitcast_fusion.1
  163.2 2.3 convolution_add_fusion.1
  165.4 0.0 all-reduce.4.cloned.1.call-update
  165.4 0.0 all-reduce.6.cloned.1.call-start
  165.5 67.5 %all-reduce.4.cloned.1.call-done = f32[3,65536]{1,0:T(4,128)} async-done(((f32[3,65536]{1,0:T(4,128)}), f32[3,65536]{1,0:T(4,128)}) %all-reduce.4.cloned.1.call-update) | async-done | bytes 786448 | tf_op jit(solution)/shard_map/psum | solution.py:73
  233.0 0.0 copy-start.1
  233.0 2.0 multiply_reduce_fusion.3
  235.0 140.8 %psum.66 = f32[3]{0:T(128)S(1)} all-reduce(f32[3]{0:T(128)S(1)} %multiply_reduce_fusion.3), channel_id=1, replica_groups=mesh['frames'=8,'atoms'=64] {'atoms'}, use_global_device_ids=true, to_apply=%region_8.0 | all-reduce | flops 3 | bytes 24 | tf_op jit(solution)/shard_map/psum | solution.py:75
  375.8 0.0 copy-done.1
  375.8 1.2 multiply_reduce_fusion.1
  377.0 142.5 %psum.67 = f32[]{:T(128)} all-reduce(f32[]{:T(128)} %multiply_reduce_fusion.1), channel_id=1, replica_groups=mesh['frames'=8,'atoms'=64] {'atoms'}, use_global_device_ids=true, to_apply=%region_10.0 | all-reduce | flops 1 | bytes 8 | tf_op jit(solution)/shard_map/psum | solution.py:76
  520.1 0.8 fusion.19
  521.0 2.3 convolution_bitcast_fusion.3
  523.4 138.0 %psum.68 = f32[1,4,3]{2,1,0:T(4,128)S(1)} all-reduce(f32[1,4,3]{2,1,0:T(4,128)S(1)} %maximum_bitcast_fusion.1), channel_id=1, replica_groups=mesh['frames'=8,'atoms'=64] {'atoms'}, use_global_device_ids=true, to_apply=%region_12.0 | all-reduce | flops 12 | bytes 96 | tf_op jit(solution)/shard_map/psum | solution.py:77
  661.4 0.2 fusion.10
  661.6 0.1 convolution_bitcast_fusion
  661.7 2.3 convolution_add_fusion
  664.0 0.0 all-reduce.6.cloned.1.call-update
  664.0 65.1 %all-reduce.6.cloned.1.call-done = f32[3,65536]{1,0:T(4,128)} async-done(((f32[3,65536]{1,0:T(4,128)}), f32[3,65536]{1,0:T(4,128)}) %all-reduce.6.cloned.1.call-update) | async-done | bytes 786448 | tf_op jit(solution)/shard_map/psum | solution.py:73
  729.1 0.0 copy-start
  729.1 2.0 multiply_reduce_fusion.2
  731.1 0.1 copy.25
  731.2 140.8 %psum.70 = f32[3]{0:T(128)S(1)} all-reduce(f32[3]{0:T(128)S(1)} %multiply_reduce_fusion.2), channel_id=1, replica_groups=mesh['frames'=8,'atoms'=64] {'atoms'}, use_global_device_ids=true, to_apply=%region_15.0 | all-reduce | flops 3 | bytes 24 | tf_op jit(solution)/shard_map/psum | solution.py:75
  872.0 0.0 copy-done
  872.0 1.2 multiply_reduce_fusion
  873.2 0.6 reshape.107
  873.8 142.5 %psum.71 = f32[]{:T(128)} all-reduce(f32[]{:T(128)} %multiply_reduce_fusion), channel_id=1, replica_groups=mesh['frames'=8,'atoms'=64] {'atoms'}, use_global_device_ids=true, to_apply=%region_17.0 | all-reduce | flops 1 | bytes 8 | tf_op jit(solution)/shard_map/psum | solution.py:76
  1017.0 1.2 subtract_divide_fusion
  (8 shorter events, 0.1 us)
Async XLA Ops:
  7.2 1.8 copy-start.2
  7.2 225.8 %all-reduce.4.cloned.1.call-start = ((), (), s32[]{:S(2)}) async-start(), calls=%async_computation | async-start | bytes 2097152 | tf_op jit(solution)/shard_map/psum | solution.py:73
  9.7 3.7 copy-start.3
  165.4 563.7 %all-reduce.6.cloned.1.call-start = ((), (), s32[]{:S(2)}) async-start(), calls=%async_computation.1 | async-start | bytes 2097152 | tf_op jit(solution)/shard_map/psum | solution.py:73
  233.0 142.8 %copy-start.1 = (f32[3,65536]{1,0:T(4,128)S(1)}, f32[3,65536]{1,0:T(4,128)}, u32[]{:S(2)}) copy-start(f32[3,65536]{1,0:T(4,128)} %all-reduce.4.cloned.1.call-done) | copy-start | bytes 2359300
  729.1 142.9 %copy-start = (f32[3,65536]{1,0:T(4,128)S(1)}, f32[3,65536]{1,0:T(4,128)}, u32[]{:S(2)}) copy-start(f32[3,65536]{1,0:T(4,128)} %all-reduce.6.cloned.1.call-done) | copy-start | bytes 2359300
Sparse Core Ops, SparseCore 0:
  165.6 67.3 all-reduce.3
  664.1 64.9 all-reduce.5
where the time goes:
time: 1030 us
  blocking collectives  851 us (83%)
  waiting for transfers between devices  133 us (13%)
  between operations  15.5 us (2%)
  other arithmetic  13.1 us (1%)
  matrix products  12 us (1%)
    psum x5, blocking collectives, per_device(): lax.psum(first, 'atoms')  705 us
    psum x1, blocking collectives, per_device(): lax.psum((gram_part, cross_part), 'atoms')  146 us
    psum x2, waiting for transfers between devices, per_device(): lax.psum(partial_sum, 'frames') / frame_count  133 us
  transfers between devices with their start and end apart: 2, of which 2 were waited for; matrix products, arithmetic and copies ran while one was open for 0% of the time, Pallas kernels for 0%

commit v1 on v0

v1 whole, which is shorter than its diff:
```python
import functools

import jax
import jax.numpy as jnp
from jax import lax
from jax.experimental import pallas as pl
from jax.experimental.pallas import tpu as pltpu
from jax.sharding import PartitionSpec as P

MESH = pl.DeviceIdType.MESH
F32, BF16 = jnp.float32, jnp.bfloat16
eps = 1e-06
FRAMES = 8
CHUNKS = 16
OFFSETS = ((2, 0), (2, 1), (1, 0), (1, 1), (3, 0), (3, 1), (0, 1), (0, 0))


def iota(shape, dim):
    return lax.broadcasted_iota(jnp.int32, shape, dim)


def split3(value):
    high = value.astype(BF16)
    rest = value - high.astype(F32)
    middle = rest.astype(BF16)
    low = (rest - middle.astype(F32)).astype(BF16)
    return high, middle, low


def kernel(ny, nz, coords, start, out, maps, xin, rin, tmp, packed, z, sums, piece,
           in_sem, send1, recv1, send2, recv2, send3, recv3, own_sem):
    frame = lax.axis_index("frames")
    block = lax.axis_index("atoms")
    x, core = frame // 2, frame % 2
    row, col = block // ny, block % ny
    share = rin.shape[1]
    tiles = share // 128
    width = share // CHUNKS
    lane_tiles = width // 128
    atom_count = float(share * FRAMES * ny * nz)

    def frame_at(k):
        dx, dc = OFFSETS[k]
        return lax.rem(x + dx, 4) * 2 + lax.rem(core + dc, 2)

    def columns(index):
        return pl.ds(pl.multiple_of(index * share, share), share)

    loads = []
    for k in range(FRAMES):
        loads.append(pltpu.make_async_copy(
            coords.at[0, :, columns(frame_at(k))], xin.at[k], in_sem.at[k]))
        loads[-1].start()
    load_start = pltpu.make_async_copy(start.at[:, columns(frame)], rin, in_sem.at[FRAMES])
    load_start.start()

    barrier = pltpu.get_barrier_semaphore()
    for k in range(FRAMES - 1):
        pl.semaphore_signal(barrier, inc=1, device_id=(frame_at(k), block), device_id_type=MESH)
    for d in range(1, ny):
        pl.semaphore_signal(
            barrier, inc=1, device_id=(frame, row * ny + lax.rem(col + d, ny)), device_id_type=MESH)
    for d in range(1, nz):
        pl.semaphore_signal(
            barrier, inc=1, device_id=(frame, lax.rem(row + d, nz) * ny + col), device_id_type=MESH)

    def spread_tiles(load):
        for t in range(tiles):
            tmp[4 * t:4 * t + 3, :] = load(t)

    def dense(j, q):
        return tmp[pl.ds(j + 4 * CHUNKS * q, CHUNKS, stride=4), :]

    own_rows = pl.ds(pl.multiple_of(frame * 3 * CHUNKS, 3 * CHUNKS), 3 * CHUNKS)
    exchange = []
    for k in range(FRAMES):
        loads[k].wait()
        spread_tiles(lambda t: xin[k, :, 128 * t:128 * (t + 1)].astype(F32))
        for j in range(3):
            for q in range(lane_tiles):
                packed[k, CHUNKS * j:CHUNKS * (j + 1), 128 * q:128 * (q + 1)] = dense(j, q).astype(BF16)
        if k == 0:
            pl.semaphore_wait(barrier, FRAMES - 1 + ny - 1 + nz - 1)
        if k < FRAMES - 1:
            exchange.append(pltpu.make_async_remote_copy(
                packed.at[k], z.at[own_rows], send1.at[k], recv1.at[k],
                device_id=(frame_at(k), block), device_id_type=MESH))
            exchange[-1].start()
    own = pltpu.make_async_copy(packed.at[FRAMES - 1], z.at[own_rows], own_sem.at[0])
    own.start()

    coord_rows = 3 * FRAMES * CHUNKS
    z[coord_rows:coord_rows + CHUNKS, :] = jnp.ones((CHUNKS, width), BF16)
    z[coord_rows + 7 * CHUNKS:coord_rows + 8 * CHUNKS, :] = jnp.zeros((CHUNKS, width), BF16)
    load_start.wait()
    spread_tiles(lambda t: rin[:, 128 * t:128 * (t + 1)])
    for j in range(3):
        for q in range(lane_tiles):
            value = dense(j, q)
            high = value.astype(BF16)
            low = (value - high.astype(F32)).astype(BF16)
            at = coord_rows + CHUNKS * (1 + j)
            z[at:at + CHUNKS, 128 * q:128 * (q + 1)] = high
            z[at + 3 * CHUNKS:at + 4 * CHUNKS, 128 * q:128 * (q + 1)] = low

    total_rows = coord_rows + 8 * CHUNKS
    group = iota((total_rows, 128), 0) >> 4
    place = jnp.where(group == 3 * FRAMES, group, (group % 3) * FRAMES + group // 3)
    collect = jnp.where(
        (place == iota((total_rows, 128), 1)) & (group <= 3 * FRAMES), 1.0, 0.0).astype(BF16)
    same_chunk = iota((CHUNKS, total_rows), 0) == (iota((CHUNKS, total_rows), 1) & (CHUNKS - 1))
    sub = iota((8, 128), 0)
    lane = iota((8, 128), 1)

    own.wait()
    for k in range(FRAMES - 1):
        exchange[k].wait_recv()

    groups = 3 * FRAMES + 7
    gram = lax.dot_general(
        z[0:groups * CHUNKS, :], z[...], (((1,), (1,)), ((), ())), preferred_element_type=F32)
    gram = jnp.where(same_chunk[None], gram.reshape(groups, CHUNKS, total_rows), 0.0)
    gram = (gram[:, :8] + gram[:, 8:]).reshape(groups * 8, total_rows)
    gram = sum(jnp.dot(part, collect, preferred_element_type=F32) for part in split3(gram))
    gram = gram.reshape(groups, 8, 128)

    def moment_row(g):
        return jnp.sum(gram[g], axis=0, keepdims=True)

    moments = jnp.zeros((8, 128), F32)
    for j in range(3):
        rows_j = jnp.zeros((8, 128), F32)
        for f in range(FRAMES):
            rows_j = jnp.where(sub == f, moment_row(3 * f + j), rows_j)
        moments = moments + (pltpu.roll(rows_j, 32 * j, 1) if j else rows_j)
    rows_3 = jnp.zeros((8, 128), F32)
    for a in range(3):
        rows_3 = jnp.where(
            (sub & 3) == a, moment_row(3 * FRAMES + 1 + a) + moment_row(3 * FRAMES + 4 + a), rows_3)
    rows_3 = jnp.where((sub & 3) == 3, moment_row(3 * FRAMES), rows_3)
    moments = moments + pltpu.roll(rows_3, 96, 1)

    sends = []
    stages = (
        (FRAMES, frame, lambda d: (lax.rem(frame + d, FRAMES), block)),
        (ny, col, lambda d: (frame, row * ny + lax.rem(col + d, ny))),
        (nz, row, lambda d: (frame, lax.rem(row + d, nz) * ny + col)),
    )
    for stage, (size, me, partner) in enumerate(stages):
        if size == 1:
            continue
        sums[stage, me] = moments
        copies = []
        for d in range(1, size):
            copies.append(pltpu.make_async_remote_copy(
                sums.at[stage, me], sums.at[stage, me], send2.at[stage, d], recv2.at[stage, d],
                device_id=partner(d), device_id_type=MESH))
            copies[-1].start()
        for copy in copies:
            copy.wait_recv()
        sends += copies
        moments = sums[stage, 0]
        for s in range(1, size):
            moments = moments + sums[stage, s]

    inside = lane < 3 * FRAMES + 1
    r = [jnp.where(inside, moments if j == 0 else pltpu.roll(moments, 128 - 32 * j, 1), 0.0) for j in range(4)]
    mean_row = r[3][3:4, :] * (1.0 / atom_count)
    at = 3 * FRAMES
    centred = [v - v[:, at:at + 1] * mean_row for v in r]

    def block_of(value, i):
        return value if i == 0 else pltpu.roll(value, 128 - FRAMES * i, 1)

    diagonal = (lane & (FRAMES - 1)) == sub
    gd = [jnp.broadcast_to(jnp.sum(jnp.where(diagonal, centred[j], 0.0), axis=0, keepdims=True), (8, 128))
          for j in range(3)]
    first = lane < FRAMES
    one = jnp.ones((8, 128), F32)
    g00, g11, g22 = (jnp.where(first, block_of(gd[j], j), one) for j in range(3))
    g01, g02, g12 = (jnp.where(first, v, 0.0) for v in (block_of(gd[0], 1), block_of(gd[0], 2), block_of(gd[1], 2)))
    i0 = 1.0 / g00
    l10, l20 = g01 * i0, g02 * i0
    i1 = 1.0 / (g11 - l10 * g01)
    t12 = g12 - l20 * g01
    l21 = t12 * i1
    i2 = 1.0 / (g22 - l20 * g02 - l21 * t12)

    def solve(c):
        y0 = c[0]
        y1 = c[1] - l10 * y0
        y2 = c[2] - l20 * y0 - l21 * y1
        x2 = y2 * i2
        x1 = y1 * i1 - l21 * x2
        x0 = y0 * i0 - l10 * x1 - l20 * x2
        return [x0, x1, x2]

    def blocks(value):
        return [jnp.where(first, block_of(value, i), 0.0) for i in range(3)]

    def cross(maps_t):
        parts = []
        for j in range(3):
            total = None
            for f in range(FRAMES):
                term = maps_t[j][:, f:f + 1] * centred[j][f:f + 1, :]
                total = term if total is None else total + term
            parts.append(total)
        return blocks(parts[0] + parts[1] + parts[2])

    used = (sub < 3) & first

    def square_mean(maps_t, crosses):
        value = sum(m * c for m, c in zip(maps_t, crosses))
        value = jnp.sum(jnp.where(used, value, 0.0), axis=0, keepdims=True)
        return jnp.sum(value, axis=1, keepdims=True) * (1.0 / atom_count)

    share_of = 1.0 / FRAMES
    m1 = [v * share_of for v in solve(blocks(centred[3]))]
    c1 = cross(m1)
    m2 = [v * share_of for v in solve(c1)]
    c2 = cross(m2)
    variance1 = square_mean(m1, c1) + eps
    variance2 = square_mean(m2, c2) + eps * variance1
    scale = 1.0 / jnp.sqrt(variance2)

    mean_blocks = blocks(jnp.broadcast_to(mean_row, (8, 128)))
    shift = -sum(m * v for m, v in zip(m2, mean_blocks))
    offset = jnp.sum(shift, axis=1, keepdims=True) * scale

    joined = m2[0] + pltpu.roll(m2[1], FRAMES, 1) + pltpu.roll(m2[2], 2 * FRAMES, 1)
    stacked = jnp.concatenate([v.astype(F32) for v in split3(joined)], axis=0).astype(BF16)
    source = iota((128, coord_rows), 1) >> 4
    expand = jnp.where((source % 3) * FRAMES + source // 3 == iota((128, coord_rows), 0), 1.0, 0.0).astype(BF16)
    wide = jnp.dot(stacked, expand, preferred_element_type=F32)
    chunk = iota((8, coord_rows), 1) & (CHUNKS - 1)
    half = iota((8, coord_rows), 0) >> 2
    lhs = jnp.concatenate(
        [jnp.where(chunk == half + 2 * rg, wide[8 * s:8 * s + 8], 0.0) for s in range(3) for rg in range(8)],
        axis=0).astype(BF16)
    aligned = jnp.dot(lhs, z[0:coord_rows, :], preferred_element_type=F32)
    aligned = aligned[0:64] + aligned[64:128] + aligned[128:192]
    for rg in range(8):
        value = aligned[8 * rg:8 * rg + 8] * scale + offset
        for h in range(2):
            for q in range(lane_tiles):
                t = q * CHUNKS + 2 * rg + h
                piece[:, 128 * t:128 * (t + 1)] = value[4 * h:4 * h + 3, 128 * q:128 * (q + 1)]

    own = pltpu.make_async_copy(piece, out.at[:, columns(frame)], own_sem.at[1])
    own.start()
    gather = []
    for k in range(FRAMES - 1):
        gather.append(pltpu.make_async_remote_copy(
            piece, out.at[:, columns(frame)], send3.at[k], recv3.at[k],
            device_id=(frame_at(k), block), device_id_type=MESH))
        gather[-1].start()

    back = FRAMES / jnp.sqrt(variance1)
    entries = [m * back for m in m2] + [shift * back]
    line = jnp.zeros((8, 128), F32)
    for j in range(4):
        value = jnp.sum(jnp.where(lane == frame, entries[j], 0.0), axis=1, keepdims=True)
        line = jnp.where((lane == 4 * sub + j) & (sub < 3), value, line)
    maps[...] = jnp.sum(line, axis=0, keepdims=True)[:, 0:12]

    own.wait()
    for copy in gather:
        copy.wait_recv()
    for copy in exchange + sends + gather:
        copy.wait_send()


def solution(mesh):
    blocks = mesh.shape["atoms"]
    ny = min(8, blocks)
    nz = blocks // ny

    def per_device(coords, start):
        atoms = start.shape[1]
        share = atoms // FRAMES
        width = share // CHUNKS
        dma = pltpu.SemaphoreType.DMA
        return pl.pallas_call(
            functools.partial(kernel, ny, nz),
            out_shape=(
                jax.ShapeDtypeStruct((3, atoms), F32),
                jax.ShapeDtypeStruct((1, 12), F32),
            ),
            in_specs=[pl.BlockSpec(memory_space=pl.ANY)] * 2,
            out_specs=(
                pl.BlockSpec(memory_space=pl.ANY),
                pl.BlockSpec(memory_space=pltpu.VMEM),
            ),
            scratch_shapes=[
                pltpu.VMEM((FRAMES, 3, share), BF16),
                pltpu.VMEM((3, share), F32),
                pltpu.VMEM((4 * (share // 128), 128), F32),
                pltpu.VMEM((FRAMES, 3 * CHUNKS, width), BF16),
                pltpu.VMEM((32 * CHUNKS, width), BF16),
                pltpu.VMEM((3, 8, 8, 128), F32),
                pltpu.VMEM((3, share), F32),
                dma((FRAMES + 1,)),
                dma((FRAMES - 1,)),
                dma((FRAMES - 1,)),
                dma((3, 8)),
                dma((3, 8)),
                dma((FRAMES - 1,)),
                dma((FRAMES - 1,)),
                dma((2,)),
            ],
            compiler_params=pltpu.CompilerParams(
                collective_id=0, has_side_effects=True, vmem_limit_bytes=32 * 1024 * 1024
            ),
        )(coords, start)

    return jax.shard_map(
        per_device,
        mesh=mesh,
        in_specs=(P("frames", None, "atoms"), P(None, "atoms")),
        out_specs=(P(None, "atoms"), P("frames", None)),
        check_vma=False,
    )
```

time: 1030 us -> 54.1 us (0.05)
  the two profiles are of different devices: /device:TPU:8 before, /device:TPU:1 now
where the time goes in v1:
time: 54.1 us; the launch traced here: 53.9 us
  Pallas kernels  49.5 us (91%)
  local copies, waits for them, and re-layouts  3.74 us (7%)
  between operations  0.65 us (1%)
    pallas_call x1, Pallas kernels, per_device(): pl.pallas_call(functools.partial(kernel, ny, nz), out_shape=(jax.ShapeDty...  49.5 us
    unnamed x6, local copies, waits for them, and re-layouts  3.74 us

profile of v1, /device:TPU:1, one launch (start us, length us, event | category | flops | bytes accessed | tf_op | source)
XLA Modules:
  0.0 53.9 jit_solution(1459873690623568428)
XLA Ops:
  0.6 0.0 copy-start
  0.6 1.2 %copy-done = f32[3,65536]{1,0:T(4,128)S(1)} copy-done((f32[3,65536]{1,0:T(4,128)S(1)}, f32[3,65536]{1,0:T(4,128)}, u32[]{:S(2)}) %copy-start) | copy-done | bytes 786456
  1.9 0.0 copy-start.1
  1.9 1.0 %copy-done.1 = bf16[1,3,65536]{2,1,0:T(4,128)(2,1)S(1)} copy-done((bf16[1,3,65536]{2,1,0:T(4,128)(2,1)S(1)}, bf16[1,3,65536]{2,1,0:T(4,128)(2,1)}, u32[]{:S(2)}) %copy-start.1) | copy-done | bytes 393240
  2.9 49.5 %shard_map.41 = (f32[3,65536]{1,0:T(4,128)S(1)}, f32[1,12]{1,0:T(1,128)S(1)}) custom-call(bf16[1,3,65536]{2,1,0:T(4,128)(2,1)S(1)} %copy-done.1, f32[3,65536]{1,0:T(4,128)S(1)} %copy-done), custom_call_target="tpu_custom_call" | custom-call | tf_op jit(solution)/shard_map/pallas_call | solution.py:284
  52.4 1.0 %copy.6 = f32[3,65536]{1,0:T(4,128)} copy(f32[3,65536]{1,0:T(4,128)S(1)} %get-tuple-element.4) | data formatting | bytes 1572864
  53.4 0.5 copy.7
Async XLA Ops:
  0.6 1.2 %copy-start = (f32[3,65536]{1,0:T(4,128)S(1)}, f32[3,65536]{1,0:T(4,128)}, u32[]{:S(2)}) copy-start(f32[3,65536]{1,0:T(4,128)} %start.1) | copy-start | bytes 2359300
  1.9 1.0 %copy-start.1 = (bf16[1,3,65536]{2,1,0:T(4,128)(2,1)S(1)}, bf16[1,3,65536]{2,1,0:T(4,128)(2,1)}, u32[]{:S(2)}) copy-start(bf16[1,3,65536]{2,1,0:T(4,128)(2,1)} %coords.1) | copy-start | bytes 1179652

commit v2 on v1

--- a/solution.py
+++ b/solution.py
@@ -27,8 +27,8 @@
     return high, middle, low
 
 
-def kernel(ny, nz, coords, start, out, maps, xin, rin, tmp, packed, z, sums, piece,
-           in_sem, send1, recv1, send2, recv2, send3, recv3, own_sem):
+def kernel(ny, nz, coords, start, out, maps, xin, rin, tmp, packed, z, others, sums, piece,
+           in_sem, send1, recv1, send2, recv2, send3, recv3, send4, recv4, own_sem, out_sem):
     frame = lax.axis_index("frames")
     block = lax.axis_index("atoms")
     x, core = frame // 2, frame % 2
@@ -46,14 +46,6 @@
     def columns(index):
         return pl.ds(pl.multiple_of(index * share, share), share)
 
-    loads = []
-    for k in range(FRAMES):
-        loads.append(pltpu.make_async_copy(
-            coords.at[0, :, columns(frame_at(k))], xin.at[k], in_sem.at[k]))
-        loads[-1].start()
-    load_start = pltpu.make_async_copy(start.at[:, columns(frame)], rin, in_sem.at[FRAMES])
-    load_start.start()
-
     barrier = pltpu.get_barrier_semaphore()
     for k in range(FRAMES - 1):
         pl.semaphore_signal(barrier, inc=1, device_id=(frame_at(k), block), device_id_type=MESH)
@@ -64,6 +56,14 @@
         pl.semaphore_signal(
             barrier, inc=1, device_id=(frame, lax.rem(row + d, nz) * ny + col), device_id_type=MESH)
 
+    loads = []
+    for k in range(FRAMES):
+        loads.append(pltpu.make_async_copy(
+            coords.at[0, :, columns(frame_at(k))], xin.at[k], in_sem.at[k]))
+        loads[-1].start()
+    load_start = pltpu.make_async_copy(start.at[:, columns(frame)], rin, in_sem.at[FRAMES])
+    load_start.start()
+
     def spread_tiles(load):
         for t in range(tiles):
             tmp[4 * t:4 * t + 3, :] = load(t)
@@ -78,16 +78,20 @@
         spread_tiles(lambda t: xin[k, :, 128 * t:128 * (t + 1)].astype(F32))
         for j in range(3):
             for q in range(lane_tiles):
-                packed[k, CHUNKS * j:CHUNKS * (j + 1), 128 * q:128 * (q + 1)] = dense(j, q).astype(BF16)
+                packed[frame_at(k), CHUNKS * j:CHUNKS * (j + 1), 128 * q:128 * (q + 1)] = dense(j, q).astype(BF16)
         if k == 0:
             pl.semaphore_wait(barrier, FRAMES - 1 + ny - 1 + nz - 1)
         if k < FRAMES - 1:
             exchange.append(pltpu.make_async_remote_copy(
-                packed.at[k], z.at[own_rows], send1.at[k], recv1.at[k],
+                packed.at[frame_at(k)], z.at[own_rows], send1.at[k], recv1.at[k],
                 device_id=(frame_at(k), block), device_id_type=MESH))
             exchange[-1].start()
-    own = pltpu.make_async_copy(packed.at[FRAMES - 1], z.at[own_rows], own_sem.at[0])
-    own.start()
+    own = [pltpu.make_async_copy(packed.at[frame], z.at[own_rows], own_sem.at[0])]
+    for m in range(1, 4):
+        own.append(pltpu.make_async_copy(
+            packed.at[lax.rem(x + m, 4) * 2 + core], others.at[m - 1, own_rows], own_sem.at[m]))
+    for copy in own:
+        copy.start()
 
     coord_rows = 3 * FRAMES * CHUNKS
     z[coord_rows:coord_rows + CHUNKS, :] = jnp.ones((CHUNKS, width), BF16)
@@ -112,7 +116,7 @@
     sub = iota((8, 128), 0)
     lane = iota((8, 128), 1)
 
-    own.wait()
+    own[0].wait()
     for k in range(FRAMES - 1):
         exchange[k].wait_recv()
 
@@ -141,21 +145,34 @@
     moments = moments + pltpu.roll(rows_3, 96, 1)
 
     sends = []
+    def far_first(size):
+        return sorted(range(1, size), key=lambda d: -min(d, size - d))
+
     stages = (
-        (FRAMES, frame, lambda d: (lax.rem(frame + d, FRAMES), block)),
-        (ny, col, lambda d: (frame, row * ny + lax.rem(col + d, ny))),
-        (nz, row, lambda d: (frame, lax.rem(row + d, nz) * ny + col)),
+        (FRAMES, frame, range(FRAMES - 1), lambda d: (frame_at(d), block)),
+        (ny, col, far_first(ny), lambda d: (frame, row * ny + lax.rem(col + d, ny))),
+        (nz, row, far_first(nz), lambda d: (frame, lax.rem(row + d, nz) * ny + col)),
     )
-    for stage, (size, me, partner) in enumerate(stages):
+    rest = []
+    for stage, (size, me, order, partner) in enumerate(stages):
         if size == 1:
             continue
         sums[stage, me] = moments
         copies = []
-        for d in range(1, size):
+        for d in order:
             copies.append(pltpu.make_async_remote_copy(
                 sums.at[stage, me], sums.at[stage, me], send2.at[stage, d], recv2.at[stage, d],
                 device_id=partner(d), device_id_type=MESH))
             copies[-1].start()
+        if stage == 0:
+            for m in range(1, 4):
+                rest.append([])
+                for k in range(FRAMES - 1):
+                    to = frame_at(k)
+                    rest[-1].append(pltpu.make_async_remote_copy(
+                        packed.at[lax.rem(to // 2 + m, 4) * 2 + to % 2], others.at[m - 1, own_rows],
+                        send3.at[m - 1, k], recv3.at[m - 1, k], device_id=(to, block), device_id_type=MESH))
+                    rest[-1][-1].start()
         for copy in copies:
             copy.wait_recv()
         sends += copies
@@ -238,23 +255,31 @@
     lhs = jnp.concatenate(
         [jnp.where(chunk == half + 2 * rg, wide[8 * s:8 * s + 8], 0.0) for s in range(3) for rg in range(8)],
         axis=0).astype(BF16)
-    aligned = jnp.dot(lhs, z[0:coord_rows, :], preferred_element_type=F32)
-    aligned = aligned[0:64] + aligned[64:128] + aligned[128:192]
-    for rg in range(8):
-        value = aligned[8 * rg:8 * rg + 8] * scale + offset
-        for h in range(2):
-            for q in range(lane_tiles):
-                t = q * CHUNKS + 2 * rg + h
-                piece[:, 128 * t:128 * (t + 1)] = value[4 * h:4 * h + 3, 128 * q:128 * (q + 1)]
-
-    own = pltpu.make_async_copy(piece, out.at[:, columns(frame)], own_sem.at[1])
-    own.start()
-    gather = []
-    for k in range(FRAMES - 1):
-        gather.append(pltpu.make_async_remote_copy(
-            piece, out.at[:, columns(frame)], send3.at[k], recv3.at[k],
-            device_id=(frame_at(k), block), device_id_type=MESH))
-        gather[-1].start()
+    placed = []
+
+    def finish(m, data):
+        aligned = jnp.dot(lhs, data, preferred_element_type=F32)
+        aligned = aligned[0:64] + aligned[64:128] + aligned[128:192]
+        for rg in range(8):
+            value = aligned[8 * rg:8 * rg + 8] * scale + offset
+            for h in range(2):
+                for q in range(lane_tiles):
+                    t = q * CHUNKS + 2 * rg + h
+                    piece[m, :, 128 * t:128 * (t + 1)] = value[4 * h:4 * h + 3, 128 * q:128 * (q + 1)]
+        target = out.at[:, columns(lax.rem(x + m, 4) * 2 + core)]
+        placed.append(pltpu.make_async_remote_copy(
+            piece.at[m], target, send4.at[m], recv4.at[m],
+            device_id=(frame_at(FRAMES - 2), block), device_id_type=MESH))
+        placed[-1].start()
+        own.append(pltpu.make_async_copy(piece.at[m], target, out_sem.at[m]))
+        own[-1].start()
+
+    finish(0, z[0:coord_rows, :])
+    for m in range(1, 4):
+        own[m].wait()
+        for copy in rest[m - 1]:
+            copy.wait_recv()
+        finish(m, others[m - 1])
 
     back = FRAMES / jnp.sqrt(variance1)
     entries = [m * back for m in m2] + [shift * back]
@@ -264,10 +289,11 @@
         line = jnp.where((lane == 4 * sub + j) & (sub < 3), value, line)
     maps[...] = jnp.sum(line, axis=0, keepdims=True)[:, 0:12]
 
-    own.wait()
-    for copy in gather:
+    for copy in own[4:]:
+        copy.wait()
+    for copy in placed:
         copy.wait_recv()
-    for copy in exchange + sends + gather:
+    for copy in exchange + sends + rest[0] + rest[1] + rest[2] + placed:
         copy.wait_send()
 
 
@@ -287,7 +313,7 @@
                 jax.ShapeDtypeStruct((3, atoms), F32),
                 jax.ShapeDtypeStruct((1, 12), F32),
             ),
-            in_specs=[pl.BlockSpec(memory_space=pl.ANY)] * 2,
+            in_specs=[pl.BlockSpec(memory_space=pltpu.HBM)] * 2,
             out_specs=(
                 pl.BlockSpec(memory_space=pl.ANY),
                 pl.BlockSpec(memory_space=pltpu.VMEM),
@@ -298,19 +324,23 @@
                 pltpu.VMEM((4 * (share // 128), 128), F32),
                 pltpu.VMEM((FRAMES, 3 * CHUNKS, width), BF16),
                 pltpu.VMEM((32 * CHUNKS, width), BF16),
+                pltpu.VMEM((3, 3 * FRAMES * CHUNKS, width), BF16),
                 pltpu.VMEM((3, 8, 8, 128), F32),
-                pltpu.VMEM((3, share), F32),
+                pltpu.VMEM((4, 3, share), F32),
                 dma((FRAMES + 1,)),
                 dma((FRAMES - 1,)),
                 dma((FRAMES - 1,)),
                 dma((3, 8)),
                 dma((3, 8)),
-                dma((FRAMES - 1,)),
-                dma((FRAMES - 1,)),
-                dma((2,)),
+                dma((3, FRAMES - 1)),
+                dma((3, FRAMES - 1)),
+                dma((4,)),
+                dma((4,)),
+                dma((4,)),
+                dma((4,)),
             ],
             compiler_params=pltpu.CompilerParams(
-                collective_id=0, has_side_effects=True, vmem_limit_bytes=32 * 1024 * 1024
+                collective_id=0, has_side_effects=True, vmem_limit_bytes=60 * 1024 * 1024
             ),
         )(coords, start)
 

time: 54.1 us -> 43.7 us (0.81)
  Pallas kernels: 49.5 us -> 40 us
  local copies, waits for them, and re-layouts: 3.74 us -> 2.89 us
    pallas_call x1, Pallas kernels: 49.5 us -> 40 us  [per_device(): pl.pallas_call(functools.partial(kernel, ny, nz), out_shape=(jax.ShapeDty...]
    unnamed x6 -> x4, local copies, waits for them, and re-layouts: 3.74 us -> 2.89 us
where the time goes in v2:
time: 43.7 us; the launch traced here: 43.6 us
  Pallas kernels  40 us (92%)
  local copies, waits for them, and re-layouts  2.89 us (7%)
  between operations  0.65 us (1%)
    pallas_call x1, Pallas kernels, per_device(): pl.pallas_call(functools.partial(kernel, ny, nz), out_shape=(jax.ShapeDty...  40 us
    unnamed x4, local copies, waits for them, and re-layouts  2.89 us

profile of v2, /device:TPU:1, one launch (start us, length us, event | category | flops | bytes accessed | tf_op | source)
XLA Modules:
  0.0 43.6 jit_solution(11225756249590598640)
XLA Ops:
  0.6 40.0 %shard_map.41 = (f32[3,65536]{1,0:T(4,128)}, f32[1,12]{1,0:T(1,128)}) custom-call(bf16[1,3,65536]{2,1,0:T(4,128)(2,1)} %coords.1, f32[3,65536]{1,0:T(4,128)} %start.1), custom_call_target="tpu_custom_call" | custom-call | tf_op jit(solution)/shard_map/pallas_call | solution.py:310
  40.7 0.0 copy-start
  40.7 2.4 %copy.6 = f32[3,65536]{1,0:T(4,128)} copy(f32[3,65536]{1,0:T(4,128)} %get-tuple-element.4) | data formatting | bytes 1572864
  43.1 0.0 copy-done
  43.1 0.5 %copy.7 = f32[1,12]{1,0:T(1,128)} copy(f32[1,12]{1,0:T(1,128)S(1)} %copy-done) | data formatting | bytes 96
Async XLA Ops:
  40.7 2.4 %copy-start = (f32[1,12]{1,0:T(1,128)S(1)}, f32[1,12]{1,0:T(1,128)}, u32[]{:S(2)}) copy-start(f32[1,12]{1,0:T(1,128)} %get-tuple-element.5) | copy-start | bytes 148

commit v3 on v2

--- a/solution.py
+++ b/solution.py
@@ -27,8 +27,8 @@
     return high, middle, low
 
 
-def kernel(ny, nz, coords, start, out, maps, xin, rin, tmp, packed, z, others, sums, piece,
-           in_sem, send1, recv1, send2, recv2, send3, recv3, send4, recv4, own_sem, out_sem):
+def kernel(ny, nz, coords, start, out, maps, xin, rin, tmp, packed, z, others, far, sums,
+           in_sem, send1, recv1, send2, recv2, send3, recv3, send4, recv4, own_sem):
     frame = lax.axis_index("frames")
     block = lax.axis_index("atoms")
     x, core = frame // 2, frame % 2
@@ -153,6 +153,10 @@
         (ny, col, far_first(ny), lambda d: (frame, row * ny + lax.rem(col + d, ny))),
         (nz, row, far_first(nz), lambda d: (frame, lax.rem(row + d, nz) * ny + col)),
     )
+    sibling = (frame_at(FRAMES - 2), block)
+    passed = [pltpu.make_async_remote_copy(
+        z.at[0:coord_rows], far.at[0], send4.at[0], recv4.at[0], device_id=sibling, device_id_type=MESH)]
+    last = 2 if nz > 1 else 1
     rest = []
     for stage, (size, me, order, partner) in enumerate(stages):
         if size == 1:
@@ -165,6 +169,7 @@
                 device_id=partner(d), device_id_type=MESH))
             copies[-1].start()
         if stage == 0:
+            passed[0].start()
             for m in range(1, 4):
                 rest.append([])
                 for k in range(FRAMES - 1):
@@ -173,6 +178,14 @@
                         packed.at[lax.rem(to // 2 + m, 4) * 2 + to % 2], others.at[m - 1, own_rows],
                         send3.at[m - 1, k], recv3.at[m - 1, k], device_id=(to, block), device_id_type=MESH))
                     rest[-1][-1].start()
+        if stage == last:
+            for m in range(1, 4):
+                own[m].wait()
+                for copy in rest[m - 1]:
+                    copy.wait_recv()
+                passed.append(pltpu.make_async_remote_copy(
+                    others.at[m - 1], far.at[m], send4.at[m], recv4.at[m], device_id=sibling, device_id_type=MESH))
+                passed[-1].start()
         for copy in copies:
             copy.wait_recv()
         sends += copies
@@ -255,9 +268,8 @@
     lhs = jnp.concatenate(
         [jnp.where(chunk == half + 2 * rg, wide[8 * s:8 * s + 8], 0.0) for s in range(3) for rg in range(8)],
         axis=0).astype(BF16)
-    placed = []
-
-    def finish(m, data):
+    def finish(m, side, data):
+        base = pl.multiple_of((lax.rem(x + m, 4) * 2 + side) * share, share)
         aligned = jnp.dot(lhs, data, preferred_element_type=F32)
         aligned = aligned[0:64] + aligned[64:128] + aligned[128:192]
         for rg in range(8):
@@ -265,21 +277,15 @@
             for h in range(2):
                 for q in range(lane_tiles):
                     t = q * CHUNKS + 2 * rg + h
-                    piece[m, :, 128 * t:128 * (t + 1)] = value[4 * h:4 * h + 3, 128 * q:128 * (q + 1)]
-        target = out.at[:, columns(lax.rem(x + m, 4) * 2 + core)]
-        placed.append(pltpu.make_async_remote_copy(
-            piece.at[m], target, send4.at[m], recv4.at[m],
-            device_id=(frame_at(FRAMES - 2), block), device_id_type=MESH))
-        placed[-1].start()
-        own.append(pltpu.make_async_copy(piece.at[m], target, out_sem.at[m]))
-        own[-1].start()
-
-    finish(0, z[0:coord_rows, :])
+                    out[:, pl.ds(pl.multiple_of(base + 128 * t, 128), 128)] = (
+                        value[4 * h:4 * h + 3, 128 * q:128 * (q + 1)])
+
+    finish(0, core, z[0:coord_rows, :])
     for m in range(1, 4):
-        own[m].wait()
-        for copy in rest[m - 1]:
-            copy.wait_recv()
-        finish(m, others[m - 1])
+        finish(m, core, others[m - 1])
+    for m in range(4):
+        passed[m].wait_recv()
+        finish(m, 1 - core, far[m])
 
     back = FRAMES / jnp.sqrt(variance1)
     entries = [m * back for m in m2] + [shift * back]
@@ -289,11 +295,7 @@
         line = jnp.where((lane == 4 * sub + j) & (sub < 3), value, line)
     maps[...] = jnp.sum(line, axis=0, keepdims=True)[:, 0:12]
 
-    for copy in own[4:]:
-        copy.wait()
-    for copy in placed:
-        copy.wait_recv()
-    for copy in exchange + sends + rest[0] + rest[1] + rest[2] + placed:
+    for copy in exchange + sends + rest[0] + rest[1] + rest[2] + passed:
         copy.wait_send()
 
 
@@ -301,6 +303,9 @@
     blocks = mesh.shape["atoms"]
     ny = min(8, blocks)
     nz = blocks // ny
+
+    def hbm(value):
+        return pltpu.with_memory_space_constraint(value, pltpu.HBM)
 
     def per_device(coords, start):
         atoms = start.shape[1]
@@ -315,7 +320,7 @@
             ),
             in_specs=[pl.BlockSpec(memory_space=pltpu.HBM)] * 2,
             out_specs=(
-                pl.BlockSpec(memory_space=pl.ANY),
+                pl.BlockSpec(memory_space=pltpu.VMEM),
                 pl.BlockSpec(memory_space=pltpu.VMEM),
             ),
             scratch_shapes=[
@@ -325,8 +330,8 @@
                 pltpu.VMEM((FRAMES, 3 * CHUNKS, width), BF16),
                 pltpu.VMEM((32 * CHUNKS, width), BF16),
                 pltpu.VMEM((3, 3 * FRAMES * CHUNKS, width), BF16),
+                pltpu.VMEM((4, 3 * FRAMES * CHUNKS, width), BF16),
                 pltpu.VMEM((3, 8, 8, 128), F32),
-                pltpu.VMEM((4, 3, share), F32),
                 dma((FRAMES + 1,)),
                 dma((FRAMES - 1,)),
                 dma((FRAMES - 1,)),
@@ -337,12 +342,11 @@
                 dma((4,)),
                 dma((4,)),
                 dma((4,)),
-                dma((4,)),
             ],
             compiler_params=pltpu.CompilerParams(
-                collective_id=0, has_side_effects=True, vmem_limit_bytes=60 * 1024 * 1024
+                collective_id=0, has_side_effects=True, vmem_limit_bytes=40 * 1024 * 1024
             ),
-        )(coords, start)
+        )(hbm(coords), hbm(start))
 
     return jax.shard_map(
         per_device,

time: 43.7 us -> 39.7 us (0.908)
  Pallas kernels: 40 us -> 37.3 us
  local copies, waits for them, and re-layouts: 2.89 us -> 1.48 us
    pallas_call x1, Pallas kernels: 40 us -> 37.3 us  [per_device(): pl.pallas_call(functools.partial(kernel, ny, nz), out_shape=(jax.ShapeDty...]
    unnamed x4 -> x2, local copies, waits for them, and re-layouts: 2.89 us -> 1.48 us
where the time goes in v3:
time: 39.7 us; the launch traced here: 39.5 us
  Pallas kernels  37.3 us (94%)
  local copies, waits for them, and re-layouts  1.48 us (4%)
  between operations  0.64 us (2%)
    pallas_call x1, Pallas kernels, per_device(): pl.pallas_call(functools.partial(kernel, ny, nz), out_shape=(jax.ShapeDty...  37.3 us
    unnamed x2, local copies, waits for them, and re-layouts  1.48 us

profile of v3, /device:TPU:1, one launch (start us, length us, event | category | flops | bytes accessed | tf_op | source)
XLA Modules:
  0.0 39.5 jit_solution(654911048161952918)
XLA Ops:
  0.6 37.3 %shard_map.41 = (f32[3,65536]{1,0:T(4,128)S(1)}, f32[1,12]{1,0:T(1,128)S(1)}) custom-call(bf16[1,3,65536]{2,1,0:T(4,128)(2,1)} %coords.1, f32[3,65536]{1,0:T(4,128)} %start.1), custom_call_target="tpu_custom_call" | custom-call | tf_op jit(solution)/shard_map/pallas_call | solution.py:315
  38.0 1.0 %copy.6 = f32[3,65536]{1,0:T(4,128)} copy(f32[3,65536]{1,0:T(4,128)S(1)} %get-tuple-element.4) | data formatting | bytes 1572864
  39.0 0.5 %copy.7 = f32[1,12]{1,0:T(1,128)} copy(f32[1,12]{1,0:T(1,128)S(1)} %get-tuple-element.5) | data formatting | bytes 96

commit v4 on v3

--- a/solution.py
+++ b/solution.py
@@ -12,7 +12,7 @@
 eps = 1e-06
 FRAMES = 8
 CHUNKS = 16
-OFFSETS = ((2, 0), (2, 1), (1, 0), (1, 1), (3, 0), (3, 1), (0, 1), (0, 0))
+OFFSETS = ((2, 0), (1, 0), (3, 0), (2, 1), (1, 1), (3, 1), (0, 1), (0, 0))
 
 
 def iota(shape, dim):
@@ -27,7 +27,7 @@
     return high, middle, low
 
 
-def kernel(ny, nz, coords, start, out, maps, xin, rin, tmp, packed, z, others, far, sums,
+def kernel(ny, nz, coords, start, out, maps, xin, rin, tmp, packed, z, folded, others, far, sums,
            in_sem, send1, recv1, send2, recv2, send3, recv3, send4, recv4, own_sem):
     frame = lax.axis_index("frames")
     block = lax.axis_index("atoms")
@@ -41,20 +41,23 @@
 
     def frame_at(k):
         dx, dc = OFFSETS[k]
-        return lax.rem(x + dx, 4) * 2 + lax.rem(core + dc, 2)
+        return lax.rem(x + dx + core * (4 - 2 * dx), 4) * 2 + lax.rem(core + dc, 2)
 
     def columns(index):
         return pl.ds(pl.multiple_of(index * share, share), share)
 
+    def far_first(size):
+        return sorted(range(1, size), key=lambda d: -min(d, size - d))
+
     barrier = pltpu.get_barrier_semaphore()
+    for d in far_first(nz):
+        pl.semaphore_signal(
+            barrier, inc=1, device_id=(frame, lax.rem(row + d, nz) * ny + col), device_id_type=MESH)
+    for d in far_first(ny):
+        pl.semaphore_signal(
+            barrier, inc=1, device_id=(frame, row * ny + lax.rem(col + d, ny)), device_id_type=MESH)
     for k in range(FRAMES - 1):
         pl.semaphore_signal(barrier, inc=1, device_id=(frame_at(k), block), device_id_type=MESH)
-    for d in range(1, ny):
-        pl.semaphore_signal(
-            barrier, inc=1, device_id=(frame, row * ny + lax.rem(col + d, ny)), device_id_type=MESH)
-    for d in range(1, nz):
-        pl.semaphore_signal(
-            barrier, inc=1, device_id=(frame, lax.rem(row + d, nz) * ny + col), device_id_type=MESH)
 
     loads = []
     for k in range(FRAMES):
@@ -94,25 +97,26 @@
         copy.start()
 
     coord_rows = 3 * FRAMES * CHUNKS
-    z[coord_rows:coord_rows + CHUNKS, :] = jnp.ones((CHUNKS, width), BF16)
-    z[coord_rows + 7 * CHUNKS:coord_rows + 8 * CHUNKS, :] = jnp.zeros((CHUNKS, width), BF16)
     load_start.wait()
     spread_tiles(lambda t: rin[:, 128 * t:128 * (t + 1)])
-    for j in range(3):
-        for q in range(lane_tiles):
-            value = dense(j, q)
-            high = value.astype(BF16)
-            low = (value - high.astype(F32)).astype(BF16)
-            at = coord_rows + CHUNKS * (1 + j)
-            z[at:at + CHUNKS, 128 * q:128 * (q + 1)] = high
-            z[at + 3 * CHUNKS:at + 4 * CHUNKS, 128 * q:128 * (q + 1)] = low
-
-    total_rows = coord_rows + 8 * CHUNKS
-    group = iota((total_rows, 128), 0) >> 4
+    for q in range(lane_tiles):
+        values = [dense(j, q) for j in range(3)]
+        highs = [value.astype(BF16).astype(F32) for value in values]
+        lows = [value - high for value, high in zip(values, highs)]
+        rows = [jnp.ones((CHUNKS, 128), F32)] + highs + lows + [jnp.zeros((CHUNKS, 128), F32)]
+        for n in range(4):
+            for h in range(2):
+                pair = jnp.concatenate([v[8 * h:8 * h + 8] for v in rows[2 * n:2 * n + 2]], axis=0)
+                at = coord_rows // 2 + CHUNKS * n
+                folded[at:at + CHUNKS, h * width + 128 * q:h * width + 128 * (q + 1)] = pair.astype(BF16)
+
+    groups = 3 * FRAMES + 8
+    total_rows = groups * 8
+    group = iota((total_rows, 128), 0) >> 3
     place = jnp.where(group == 3 * FRAMES, group, (group % 3) * FRAMES + group // 3)
     collect = jnp.where(
         (place == iota((total_rows, 128), 1)) & (group <= 3 * FRAMES), 1.0, 0.0).astype(BF16)
-    same_chunk = iota((CHUNKS, total_rows), 0) == (iota((CHUNKS, total_rows), 1) & (CHUNKS - 1))
+    same_chunk = iota((8, total_rows), 0) == (iota((8, total_rows), 1) & 7)
     sub = iota((8, 128), 0)
     lane = iota((8, 128), 1)
 
@@ -120,11 +124,14 @@
     for k in range(FRAMES - 1):
         exchange[k].wait_recv()
 
-    groups = 3 * FRAMES + 7
+    for n in range(3 * FRAMES // 2):
+        pair = [z[CHUNKS * g:CHUNKS * (g + 1), :].astype(F32) for g in (2 * n, 2 * n + 1)]
+        for h in range(2):
+            folded[CHUNKS * n:CHUNKS * (n + 1), h * width:(h + 1) * width] = jnp.concatenate(
+                [v[8 * h:8 * h + 8] for v in pair], axis=0).astype(BF16)
     gram = lax.dot_general(
-        z[0:groups * CHUNKS, :], z[...], (((1,), (1,)), ((), ())), preferred_element_type=F32)
-    gram = jnp.where(same_chunk[None], gram.reshape(groups, CHUNKS, total_rows), 0.0)
-    gram = (gram[:, :8] + gram[:, 8:]).reshape(groups * 8, total_rows)
+        folded[...], folded[...], (((1,), (1,)), ((), ())), preferred_element_type=F32)
+    gram = jnp.where(same_chunk[None], gram.reshape(groups, 8, total_rows), 0.0).reshape(total_rows, total_rows)
     gram = sum(jnp.dot(part, collect, preferred_element_type=F32) for part in split3(gram))
     gram = gram.reshape(groups, 8, 128)
 
@@ -145,9 +152,6 @@
     moments = moments + pltpu.roll(rows_3, 96, 1)
 
     sends = []
-    def far_first(size):
-        return sorted(range(1, size), key=lambda d: -min(d, size - d))
-
     stages = (
         (FRAMES, frame, range(FRAMES - 1), lambda d: (frame_at(d), block)),
         (ny, col, far_first(ny), lambda d: (frame, row * ny + lax.rem(col + d, ny))),
@@ -155,7 +159,7 @@
     )
     sibling = (frame_at(FRAMES - 2), block)
     passed = [pltpu.make_async_remote_copy(
-        z.at[0:coord_rows], far.at[0], send4.at[0], recv4.at[0], device_id=sibling, device_id_type=MESH)]
+        z, far.at[0], send4.at[0], recv4.at[0], device_id=sibling, device_id_type=MESH)]
     last = 2 if nz > 1 else 1
     rest = []
     for stage, (size, me, order, partner) in enumerate(stages):
@@ -280,7 +284,7 @@
                     out[:, pl.ds(pl.multiple_of(base + 128 * t, 128), 128)] = (
                         value[4 * h:4 * h + 3, 128 * q:128 * (q + 1)])
 
-    finish(0, core, z[0:coord_rows, :])
+    finish(0, core, z[...])
     for m in range(1, 4):
         finish(m, core, others[m - 1])
     for m in range(4):
@@ -328,7 +332,8 @@
                 pltpu.VMEM((3, share), F32),
                 pltpu.VMEM((4 * (share // 128), 128), F32),
                 pltpu.VMEM((FRAMES, 3 * CHUNKS, width), BF16),
-                pltpu.VMEM((32 * CHUNKS, width), BF16),
+                pltpu.VMEM((3 * FRAMES * CHUNKS, width), BF16),
+                pltpu.VMEM((32 * 8, 2 * width), BF16),
                 pltpu.VMEM((3, 3 * FRAMES * CHUNKS, width), BF16),
                 pltpu.VMEM((4, 3 * FRAMES * CHUNKS, width), BF16),
                 pltpu.VMEM((3, 8, 8, 128), F32),

time: 39.7 us -> 39 us (0.982)
  Pallas kernels: 37.3 us -> 36.7 us
    pallas_call x1, Pallas kernels: 37.3 us -> 36.7 us  [per_device(): pl.pallas_call(functools.partial(kernel, ny, nz), out_shape=(jax.ShapeDty...]
where the time goes in v4:
time: 39 us; the launch traced here: 38.9 us
  Pallas kernels  36.7 us (94%)
  local copies, waits for them, and re-layouts  1.48 us (4%)
  between operations  0.64 us (2%)
    pallas_call x1, Pallas kernels, per_device(): pl.pallas_call(functools.partial(kernel, ny, nz), out_shape=(jax.ShapeDty...  36.7 us
    unnamed x2, local copies, waits for them, and re-layouts  1.48 us

profile of v4, /device:TPU:1, one launch (start us, length us, event | category | flops | bytes accessed | tf_op | source)
XLA Modules:
  0.0 38.9 jit_solution(15502405749219415448)
XLA Ops:
  0.6 36.7 %shard_map.41 = (f32[3,65536]{1,0:T(4,128)S(1)}, f32[1,12]{1,0:T(1,128)S(1)}) custom-call(bf16[1,3,65536]{2,1,0:T(4,128)(2,1)} %coords.1, f32[3,65536]{1,0:T(4,128)} %start.1), custom_call_target="tpu_custom_call" | custom-call | tf_op jit(solution)/shard_map/pallas_call | solution.py:319
  37.4 1.0 %copy.6 = f32[3,65536]{1,0:T(4,128)} copy(f32[3,65536]{1,0:T(4,128)S(1)} %get-tuple-element.4) | data formatting | bytes 1572864
  38.4 0.5 %copy.7 = f32[1,12]{1,0:T(1,128)} copy(f32[1,12]{1,0:T(1,128)S(1)} %get-tuple-element.5) | data formatting | bytes 96

commit v5 on v4

--- a/solution.py
+++ b/solution.py
@@ -28,7 +28,7 @@
 
 
 def kernel(ny, nz, coords, start, out, maps, xin, rin, tmp, packed, z, folded, others, far, sums,
-           in_sem, send1, recv1, send2, recv2, send3, recv3, send4, recv4, own_sem):
+           in_sem, send1, recv1, send2, recv2, send3, recv3, send4, recv4, own_sem, send6, recv6):
     frame = lax.axis_index("frames")
     block = lax.axis_index("atoms")
     x, core = frame // 2, frame % 2
@@ -74,7 +74,10 @@
     def dense(j, q):
         return tmp[pl.ds(j + 4 * CHUNKS * q, CHUNKS, stride=4), :]
 
-    own_rows = pl.ds(pl.multiple_of(frame * 3 * CHUNKS, 3 * CHUNKS), 3 * CHUNKS)
+    def rows_of(index):
+        return pl.ds(pl.multiple_of(index * 3 * CHUNKS, 3 * CHUNKS), 3 * CHUNKS)
+
+    own_rows = rows_of(frame)
     exchange = []
     for k in range(FRAMES):
         loads[k].wait()
@@ -162,6 +165,26 @@
         z, far.at[0], send4.at[0], recv4.at[0], device_id=sibling, device_id_type=MESH)]
     last = 2 if nz > 1 else 1
     rest = []
+    from_low = rows_of(lax.rem(x + 3, 4) * 2)
+    from_high = rows_of(lax.rem(x + 1, 4) * 2 + 1)
+    low, high = lax.rem(x + 3, 4) * 2 + core, lax.rem(x + 1, 4) * 2 + core
+    relays = []
+    for n, (source, m, rows, to) in enumerate((
+            (z.at[from_low], 3, from_low, high),
+            (z.at[from_high], 1, from_high, low),
+            (others.at[1, from_low], 1, from_low, high),
+            (others.at[2, from_low], 2, from_low, high),
+            (others.at[0, from_high], 2, from_high, low),
+            (others.at[1, from_high], 3, from_high, low))):
+        relays.append(pltpu.make_async_remote_copy(
+            source, others.at[m - 1, rows], send6.at[n], recv6.at[n], device_id=(to, block), device_id_type=MESH))
+
+    def arrived(m, k):
+        pltpu.make_async_remote_copy(
+            packed.at[0], others.at[m - 1, own_rows], send3.at[m - 1, k], recv3.at[m - 1, k],
+            device_id=sibling, device_id_type=MESH).wait_recv()
+
+    low_k, high_k = 1 + 3 * core, 1 + 3 * (1 - core)
     for stage, (size, me, order, partner) in enumerate(stages):
         if size == 1:
             continue
@@ -174,19 +197,31 @@
             copies[-1].start()
         if stage == 0:
             passed[0].start()
-            for m in range(1, 4):
-                rest.append([])
-                for k in range(FRAMES - 1):
-                    to = frame_at(k)
-                    rest[-1].append(pltpu.make_async_remote_copy(
-                        packed.at[lax.rem(to // 2 + m, 4) * 2 + to % 2], others.at[m - 1, own_rows],
-                        send3.at[m - 1, k], recv3.at[m - 1, k], device_id=(to, block), device_id_type=MESH))
-                    rest[-1][-1].start()
+            order = [(m, k) for m in (2, 3 - 2 * core) for k in (1, 4)]
+            order += [(m, k) for m in (1, 2, 3) for k in (2, 5, 6)]
+            order += [(1 + 2 * core, k) for k in (1, 4)]
+            for m, k in order:
+                to = frame_at(k)
+                rest.append(pltpu.make_async_remote_copy(
+                    packed.at[lax.rem(to // 2 + m, 4) * 2 + to % 2], others.at[m - 1, own_rows],
+                    send3.at[m - 1, k], recv3.at[m - 1, k], device_id=(to, block), device_id_type=MESH))
+                rest[-1].start()
+            for copy in relays[:2]:
+                copy.start()
+        if stage == 1:
+            for m, k in ((2, low_k), (3, low_k), (1, high_k), (2, high_k)):
+                arrived(m, k)
+            for copy in relays[2:]:
+                copy.start()
         if stage == last:
-            for m in range(1, 4):
+            arrived(1, low_k)
+            arrived(3, high_k)
+            for m, via in ((1, (1, 2)), (2, (3, 4)), (3, (0, 5))):
                 own[m].wait()
-                for copy in rest[m - 1]:
-                    copy.wait_recv()
+                for k in (2, 5, 6):
+                    arrived(m, k)
+                for n in via:
+                    relays[n].wait_recv()
                 passed.append(pltpu.make_async_remote_copy(
                     others.at[m - 1], far.at[m], send4.at[m], recv4.at[m], device_id=sibling, device_id_type=MESH))
                 passed[-1].start()
@@ -299,7 +334,7 @@
         line = jnp.where((lane == 4 * sub + j) & (sub < 3), value, line)
     maps[...] = jnp.sum(line, axis=0, keepdims=True)[:, 0:12]
 
-    for copy in exchange + sends + rest[0] + rest[1] + rest[2] + passed:
+    for copy in exchange + sends + rest + relays + passed:
         copy.wait_send()
 
 
@@ -347,6 +382,8 @@
                 dma((4,)),
                 dma((4,)),
                 dma((4,)),
+                dma((6,)),
+                dma((6,)),
             ],
             compiler_params=pltpu.CompilerParams(
                 collective_id=0, has_side_effects=True, vmem_limit_bytes=40 * 1024 * 1024

time: 39 us -> 38.5 us (0.987)
  Pallas kernels: 36.7 us -> 36.3 us
    pallas_call x1, Pallas kernels: 36.7 us -> 36.3 us  [per_device(): pl.pallas_call(functools.partial(kernel, ny, nz), out_shape=(jax.ShapeDty...]
where the time goes in v5:
time: 38.5 us; the launch traced here: 38.4 us
  Pallas kernels  36.3 us (94%)
  local copies, waits for them, and re-layouts  1.48 us (4%)
  between operations  0.64 us (2%)
    pallas_call x1, Pallas kernels, per_device(): pl.pallas_call(functools.partial(kernel, ny, nz), out_shape=(jax.ShapeDty...  36.3 us
    unnamed x2, local copies, waits for them, and re-layouts  1.48 us

profile of v5, /device:TPU:1, one launch (start us, length us, event | category | flops | bytes accessed | tf_op | source)
XLA Modules:
  0.0 38.4 jit_solution(15487704876207033716)
XLA Ops:
  0.6 36.3 %shard_map.41 = (f32[3,65536]{1,0:T(4,128)S(1)}, f32[1,12]{1,0:T(1,128)S(1)}) custom-call(bf16[1,3,65536]{2,1,0:T(4,128)(2,1)} %coords.1, f32[3,65536]{1,0:T(4,128)} %start.1), custom_call_target="tpu_custom_call" | custom-call | tf_op jit(solution)/shard_map/pallas_call | solution.py:354
  36.9 1.0 %copy.6 = f32[3,65536]{1,0:T(4,128)} copy(f32[3,65536]{1,0:T(4,128)S(1)} %get-tuple-element.4) | data formatting | bytes 1572864
  37.9 0.5 %copy.7 = f32[1,12]{1,0:T(1,128)} copy(f32[1,12]{1,0:T(1,128)S(1)} %get-tuple-element.5) | data formatting | bytes 96

commit v6 on v5

--- a/solution.py
+++ b/solution.py
@@ -135,7 +135,8 @@
     gram = lax.dot_general(
         folded[...], folded[...], (((1,), (1,)), ((), ())), preferred_element_type=F32)
     gram = jnp.where(same_chunk[None], gram.reshape(groups, 8, total_rows), 0.0).reshape(total_rows, total_rows)
-    gram = sum(jnp.dot(part, collect, preferred_element_type=F32) for part in split3(gram))
+    gram = jnp.dot(jnp.concatenate(split3(gram), axis=0), collect, preferred_element_type=F32)
+    gram = gram[:total_rows] + gram[total_rows:2 * total_rows] + gram[2 * total_rows:]
     gram = gram.reshape(groups, 8, 128)
 
     def moment_row(g):

time: 38.5 us -> 38.5 us (level)
  no operation moved by 1% of the time
where the time goes in v6:
time: 38.5 us; the launch traced here: 38.4 us
  Pallas kernels  36.3 us (94%)
  local copies, waits for them, and re-layouts  1.48 us (4%)
  between operations  0.64 us (2%)
    pallas_call x1, Pallas kernels, per_device(): pl.pallas_call(functools.partial(kernel, ny, nz), out_shape=(jax.ShapeDty...  36.3 us
    unnamed x2, local copies, waits for them, and re-layouts  1.48 us

profile of v6, /device:TPU:1, one launch (start us, length us, event | category | flops | bytes accessed | tf_op | source)
XLA Modules:
  0.0 38.4 jit_solution(8997629596641987464)
XLA Ops:
  0.6 36.3 %shard_map.41 = (f32[3,65536]{1,0:T(4,128)S(1)}, f32[1,12]{1,0:T(1,128)S(1)}) custom-call(bf16[1,3,65536]{2,1,0:T(4,128)(2,1)} %coords.1, f32[3,65536]{1,0:T(4,128)} %start.1), custom_call_target="tpu_custom_call" | custom-call | tf_op jit(solution)/shard_map/pallas_call | solution.py:355
  36.9 1.0 %copy.6 = f32[3,65536]{1,0:T(4,128)} copy(f32[3,65536]{1,0:T(4,128)S(1)} %get-tuple-element.4) | data formatting | bytes 1572864
  37.9 0.5 %copy.7 = f32[1,12]{1,0:T(1,128)} copy(f32[1,12]{1,0:T(1,128)S(1)} %get-tuple-element.5) | data formatting | bytes 96

commit v7 on v5

--- a/solution.py
+++ b/solution.py
@@ -157,8 +157,8 @@
     sends = []
     stages = (
         (FRAMES, frame, range(FRAMES - 1), lambda d: (frame_at(d), block)),
+        (nz, row, far_first(nz), lambda d: (frame, lax.rem(row + d, nz) * ny + col)),
         (ny, col, far_first(ny), lambda d: (frame, row * ny + lax.rem(col + d, ny))),
-        (nz, row, far_first(nz), lambda d: (frame, lax.rem(row + d, nz) * ny + col)),
     )
     sibling = (frame_at(FRAMES - 2), block)
     passed = [pltpu.make_async_remote_copy(

time: 38.5 us -> 38.5 us (level)
  no operation moved by 1% of the time
where the time goes in v7:
time: 38.5 us; the launch traced here: 38.4 us
  Pallas kernels  36.3 us (94%)
  local copies, waits for them, and re-layouts  1.48 us (4%)
  between operations  0.64 us (2%)
    pallas_call x1, Pallas kernels, per_device(): pl.pallas_call(functools.partial(kernel, ny, nz), out_shape=(jax.ShapeDty...  36.3 us
    unnamed x2, local copies, waits for them, and re-layouts  1.48 us

profile of v7, /device:TPU:1, one launch (start us, length us, event | category | flops | bytes accessed | tf_op | source)
XLA Modules:
  0.0 38.4 jit_solution(10302028464240174024)
XLA Ops:
  0.6 36.3 %shard_map.41 = (f32[3,65536]{1,0:T(4,128)S(1)}, f32[1,12]{1,0:T(1,128)S(1)}) custom-call(bf16[1,3,65536]{2,1,0:T(4,128)(2,1)} %coords.1, f32[3,65536]{1,0:T(4,128)} %start.1), custom_call_target="tpu_custom_call" | custom-call | tf_op jit(solution)/shard_map/pallas_call | solution.py:354
  36.9 1.0 %copy.6 = f32[3,65536]{1,0:T(4,128)} copy(f32[3,65536]{1,0:T(4,128)S(1)} %get-tuple-element.4) | data formatting | bytes 1572864
  37.9 0.5 %copy.7 = f32[1,12]{1,0:T(1,128)} copy(f32[1,12]{1,0:T(1,128)S(1)} %get-tuple-element.5) | data formatting | bytes 96
